TPU v7x, 1024 devices: a whole 4x4x32 slice. The times are simulated.
1024 devices in a mesh: row: 32 (over x, y, core), col: 32 (over z).
Axes of the slice: x: 4, y: 4, z: 32, core: 2. Of those that a mesh axis runs over, the one named last changes fastest.
Arguments:
- values: bfloat16 [32, 32, 10, 64, 64], P('row', 'col'), may hold values from -0.59765625 to 0.59765625
- block_rows: int32 [32, 32, 10], P('row', 'col'), may hold values from -1 to 1279, as said below
- block_cols: int32 [32, 32, 10], P('row', 'col'), may hold values from -1 to 1279, as said below
Outputs:
- purified: float32 [32, 32, 10, 64, 64], P('row', 'col')
Inputs may be any that keep to these rules, and one draw needn't show every extreme that they name: `block_rows`: tile (i, j) holds only blocks whose row lies in [i * 40, (i + 1) * 40) and whose column lies in [j * 40, (j + 1) * 40); live slots come first and empty ones hold -1; no block is stored twice; a block row holds at most 7 blocks. `block_cols`: empty slots hold -1 here exactly where block_rows does.
All inputs are finite; a program needn't handle non-finite values.
Results may differ from a plain program's by a relative error of at most 0.0021.
Values may be sent and summed in bfloat16 or wider, within the bound.
A program may use at most 32 MiB of HBM per device.

v0:
```python
import jax
import jax.numpy as jnp
from jax import lax
from jax.sharding import PartitionSpec as P

NEIGH = 7


def select_pairs(left_rows, left_cols, right_rows, right_cols, out_rows, out_cols):
    left_count = left_rows.shape[0]
    right_count = right_rows.shape[0]
    same_row = (left_rows[None, :] == out_rows[:, None]) & (left_rows[None, :] >= 0)
    linked = (
        (right_rows[None, None, :] == left_cols[None, :, None])
        & (right_cols[None, None, :] == out_cols[:, None, None])
        & (right_rows[None, None, :] >= 0)
    )
    found = jnp.any(linked, axis=2)
    partner = jnp.sum(
        jnp.where(linked, jnp.arange(right_count, dtype=jnp.int32)[None, None, :], 0), axis=2
    )
    valid = same_row & found
    scores = jnp.where(valid, left_count - jnp.arange(left_count, dtype=jnp.int32)[None, :], 0)
    top_scores, chosen = lax.top_k(scores, min(NEIGH, left_count))
    paired = jnp.take_along_axis(partner, chosen, axis=1)
    return (chosen, paired, top_scores > 0)


def block_product(left_sel, right_sel, keep):
    left_sel = jnp.where(keep[:, :, None, None], left_sel, jnp.zeros((), left_sel.dtype))
    return jnp.einsum("opik,opkj->oij", left_sel, right_sel, preferred_element_type=jnp.float32)


def shards(values, block_rows, block_cols):
    tile_vals = values.reshape(values.shape[2:])
    tile_rows = block_rows.reshape(-1)
    tile_cols = block_cols.reshape(-1)
    panel_vals, panel_rows, panel_cols = (
        lax.all_gather(tile_vals, "col", axis=0, tiled=True),
        lax.all_gather(tile_rows, "col", axis=0, tiled=True),
        lax.all_gather(tile_cols, "col", axis=0, tiled=True),
    )
    column_vals, column_rows, column_cols = (
        lax.all_gather(tile_vals, "row", axis=0, tiled=True),
        lax.all_gather(tile_rows, "row", axis=0, tiled=True),
        lax.all_gather(tile_cols, "row", axis=0, tiled=True),
    )
    chosen, paired, keep = select_pairs(
        panel_rows, panel_cols, column_rows, column_cols, tile_rows, tile_cols
    )
    right_sel = column_vals[paired]
    square = block_product(panel_vals[chosen], right_sel, keep)
    square_sent = square.astype(jnp.bfloat16)
    square_panel = lax.all_gather(square_sent, "col", axis=0, tiled=True)
    left_sel = square_panel[chosen]
    cube = block_product(left_sel, right_sel, keep)
    live = (tile_rows >= 0)[:, None, None]
    purified = jnp.where(live, 3.0 * square - 2.0 * cube, 0.0)
    return purified.reshape(values.shape)


def solution(mesh):
    in_specs = (P("row", "col", None, None, None), P("row", "col", None), P("row", "col", None))
    out_specs = P("row", "col", None, None, None)
    return jax.shard_map(shards, mesh=mesh, in_specs=in_specs, out_specs=out_specs, check_vma=False)
```

profile of v0, /device:TPU:12, one launch (start us, length us, event | category | flops | bytes accessed | tf_op | source)
XLA Modules:
  0.0 406.9 jit_solution(12374147865917546710)
XLA Ops:
  6.5 0.7 all-gather.14.cloned.1.call-update
  7.3 0.7 all-gather.12.cloned.1.call-update
  8.0 0.0 all-gather.10.cloned.1.call-start
  8.1 1.3 dynamic-slice.1
  9.3 1.3 dynamic-slice
  12.0 0.8 bitcast_dynamic-update-slice_fusion
  12.7 0.7 bitcast_dynamic-update-slice_fusion.2
  13.5 18.7 %all-reduce.5 = (s32[320]{0:T(512)S(1)}, s32[320]{0:T(512)S(1)}) all-reduce(s32[320]{0:T(512)S(1)} %bitcast_dynamic-update-slice_fusion.2, s32[320]{0:T(512)S(1)} %bitcast_dynamic-update-slice_fusion), channel_id=3, replica_groups=mesh['row'=32,'col'=32] {'row'}, use_global_device_ids=true, to_apply=%add.1 | all-reduce | flops 640 | bytes 5120 | tf_op jit(solution)/shard_map/all_gather | solution.py:45
  32.2 0.7 bitcast_dynamic-update-slice_fusion.1
  32.9 0.7 bitcast_dynamic-update-slice_fusion.3
  33.7 40.4 %all-reduce.4 = (s32[320]{0:T(512)S(1)}, s32[320]{0:T(512)S(1)}) all-reduce(s32[320]{0:T(512)S(1)} %bitcast_dynamic-update-slice_fusion.1, s32[320]{0:T(512)S(1)} %bitcast_dynamic-update-slice_fusion.3), channel_id=4, replica_groups=mesh['row'=32,'col'=32] {'col'}, use_global_device_ids=true, to_apply=%add.2 | all-reduce | flops 640 | bytes 5120
  74.1 0.7 broadcast_compare_fusion.1
  74.8 0.1 broadcast_compare_fusion
  75.0 0.7 fusion
  75.7 0.7 and_select_fusion
  76.5 3.4 top_k.12
  79.9 0.1 copy.17
  80.0 0.1 copy.18
  80.1 0.1 reshape.131
  80.2 1.3 select_reduce_fusion
  81.4 2.1 gather_fusion.3
  83.5 0.1 reshape.134
  83.6 0.1 reshape.117
  83.7 0.1 reshape.109
  83.8 17.8 %all-gather.14.cloned.1.call-done = bf16[1,1,320,64,64]{4,3,1,0,2:T(8,128)(2,1)} async-done(((bf16[1,1,10,64,64]{4,3,1,0,2:T(8,128)(2,1)}), bf16[1,1,320,64,64]{4,3,1,0,2:T(8,128)(2,1)}) %all-gather.14.cloned.1.call-update) | async-done | bytes 2621456 | tf_op jit(solution)/shard_map/all_gather | solution.py:44
  101.6 3.3 gather_fusion.1
  104.9 148.4 %all-gather.12.cloned.1.call-done = bf16[1,1,320,64,64]{4,3,1,0,2:T(8,128)(2,1)} async-done(((bf16[1,1,10,64,64]{4,3,1,0,2:T(8,128)(2,1)}), bf16[1,1,320,64,64]{4,3,1,0,2:T(8,128)(2,1)}) %all-gather.12.cloned.1.call-update) | async-done | bytes 2621456 | tf_op jit(solution)/shard_map/all_gather | solution.py:39
  253.3 3.3 gather_fusion
  256.5 1.3 fusion.13
  257.9 137.8 %all-gather.10.cloned.1.call-done = bf16[320,64,64]{2,1,0:T(8,128)(2,1)} async-done(((bf16[10,64,64]{2,1,0:T(8,128)(2,1)}), bf16[320,64,64]{2,1,0:T(8,128)(2,1)}) %all-gather.10.cloned.1.call-update) | async-done | bytes 2621456 | tf_op jit(solution)/shard_map/all_gather | solution.py:54
  395.7 3.3 gather_fusion.2
  398.9 1.4 fusion.4
  (20 shorter events, 0.1 us)
Async XLA Ops:
  6.5 95.1 %all-gather.14.cloned.1.call-start = ((), (), s32[]{:S(2)}) async-start(), calls=%async_computation.2 | async-start | bytes 5406720 | tf_op jit(solution)/shard_map/all_gather | solution.py:44
  7.3 246.0 %all-gather.12.cloned.1.call-start = ((), (), s32[]{:S(2)}) async-start(), calls=%async_computation.1 | async-start | bytes 5406720 | tf_op jit(solution)/shard_map/all_gather | solution.py:39
  8.0 387.7 %all-gather.10.cloned.1.call-start = ((), (), s32[]{:S(2)}) async-start(), calls=%async_computation | async-start | bytes 5406720 | tf_op jit(solution)/shard_map/all_gather | solution.py:54
  256.5 1.4 copy-start
Sparse Core Ops, SparseCore 0:
  11.6 89.9 all-gather.13
  104.3 148.9 all-gather.11
  258.0 137.6 all-gather.9
where the time goes:
time: 407 us
  waiting for transfers between devices  305 us (75%)
  blocking collectives  59.1 us (15%)
  local copies, waits for them, and re-layouts  17.9 us (4%)
  between operations  14.6 us (4%)
  other arithmetic  7.06 us (2%)
    all_gather x1, waiting for transfers between devices, shards(): lax.all_gather(tile_vals, 'col', axis=0, tiled=True)  148 us
    all_gather x1, waiting for transfers between devices, shards(): square_panel = lax.all_gather(square_sent, 'col', axis=0, tiled=True)  138 us
    unnamed x1, blocking collectives  40.4 us
    all_gather x1, blocking collectives, shards(): lax.all_gather(tile_rows, 'row', axis=0, tiled=True)  18.7 us
    all_gather x1, waiting for transfers between devices, shards(): lax.all_gather(tile_vals, 'row', axis=0, tiled=True)  17.8 us
  transfers between devices with their start and end apart: 3, of which 3 were waited for; matrix products, arithmetic and copies ran while one was open for 5% of the time, Pallas kernels for 0%

commit v1 on v0

v1 whole, which is shorter than its diff:
```python
import functools

import jax
import jax.numpy as jnp
from jax import lax
from jax.experimental import pallas as pl
from jax.experimental.pallas import tpu as pltpu
from jax.sharding import PartitionSpec as P

NEIGH = 7
CAP = 10
BLK = 64
PAIRS = CAP // 2
LANES = 128
SHIFT = 11
BIG = 1 << 30
MESH = pl.DeviceIdType.MESH


def own_keys(rows, cols):
    key = jnp.where(rows >= 0, (rows << SHIFT) | cols, -1)
    slot = lax.broadcasted_iota(jnp.int32, (16, CAP), 0)
    lane = lax.broadcasted_iota(jnp.int32, (16, CAP), 1)
    column = jnp.sum(jnp.where(slot == lane, key + 1, 0), axis=1, keepdims=True) - 1
    slot = lax.broadcasted_iota(jnp.int32, (16, LANES), 0)
    lane = lax.broadcasted_iota(jnp.int32, (16, LANES), 1)
    row = jnp.sum(jnp.where(lax.rem(lane, 16) == slot, column, 0), axis=0, keepdims=True)
    return column, row


def lane_dense(meta, tiles):
    lane = lax.broadcasted_iota(jnp.int32, (1, LANES), 1) // 16
    groups = []
    for base in range(0, tiles, 8):
        group = jnp.full((1, LANES), -1, jnp.int32)
        for m in range(min(8, tiles - base)):
            group = jnp.where(lane == m, meta[base + m], group)
        groups.append(group)
    return groups


def slot_ids(groups):
    lane = lax.broadcasted_iota(jnp.int32, (1, LANES), 1)
    return [(lane // 16 + 8 * g) * CAP + lax.rem(lane, 16) for g in range(groups)]


def pair_up(mine, left, right):
    ids_left, ids_right = slot_ids(len(left)), slot_ids(len(right))
    codes = []
    for keys, ids in zip(left, ids_left):
        same = ((keys >> SHIFT) == (mine >> SHIFT)) & (keys >= 0) & (mine >= 0)
        codes.append(jnp.where(same, (ids << SHIFT) | (keys & ((1 << SHIFT) - 1)), BIG))
    column = mine & ((1 << SHIFT) - 1)
    lane = lax.broadcasted_iota(jnp.int32, (16, LANES), 1)
    chosen = jnp.full((16, LANES), -1, jnp.int32)
    paired = jnp.full((16, LANES), -1, jnp.int32)
    for n in range(NEIGH):
        least = functools.reduce(jnp.minimum, codes)
        least = jnp.min(least, axis=1, keepdims=True)
        codes = [jnp.where(code == least, BIG, code) for code in codes]
        want = ((least & ((1 << SHIFT) - 1)) << SHIFT) | column
        hits = [jnp.where(keys == want, ids, -1) for keys, ids in zip(right, ids_right)]
        partner = jnp.max(functools.reduce(jnp.maximum, hits), axis=1, keepdims=True)
        good = (least < BIG) & (partner >= 0)
        chosen = jnp.where(lane == n, jnp.where(good, least >> SHIFT, -1), chosen)
        paired = jnp.where(lane == n, jnp.where(good, partner, -1), paired)
    return chosen, paired


def swap_halves(block):
    return jnp.concatenate([block[:, BLK:], block[:, :BLK]], axis=1)


def in_half(panel, code, half):
    block = panel[jnp.maximum(code, 0) >> 1]
    return jnp.where((code & 1) == half, block, swap_halves(block))


def left_row(panel, codes, out):
    low = lax.broadcasted_iota(jnp.int32, (BLK, LANES), 1) < BLK
    chunks = []
    for n in range(0, NEIGH + 1, 2):
        halves = []
        for half in range(2):
            if n + half < NEIGH:
                code = codes[out, n + half]
                block = in_half(panel, code, half)
                halves.append(jnp.where(code >= 0, block, jnp.zeros_like(block)))
            else:
                halves.append(jnp.zeros((BLK, LANES), panel.dtype))
        chunks.append(jnp.where(low, halves[0], halves[1]))
    return jnp.concatenate(chunks, axis=1)


def right_column(panel, codes, out):
    blocks = [in_half(panel, codes[16 + out, n], 0) for n in range(NEIGH)]
    return jnp.concatenate(blocks + [blocks[-1]], axis=0)


def kernel(
    nx, ny, nz,
    values, rows, cols, out,
    left_panel, right_panel, square_panel, stacked, square,
    left_meta, right_meta, codes_vector, codes,
    left_send, left_recv, square_send, square_recv,
    plane_send, plane_recv, twin_send, twin_recv,
    meta_send, meta_recv, codes_sem,
):
    plane = nx * ny
    me, z = lax.axis_index("row"), lax.axis_index("col")
    core = lax.rem(me, 2)
    x, y = me // (2 * ny), lax.rem(me // 2, ny)
    above, below = lax.rem(z + 1, nz), lax.rem(z + nz - 1, nz)
    twin = (me + 1 - 2 * core, z)

    def at_plane(dx, dy):
        return (lax.rem(x + dx + nx, nx) * ny + lax.rem(y + dy + ny, ny)) * 2 + core, z

    def at_depth(dz):
        return me, lax.rem(z + dz + nz, nz)

    z_steps = [1 << k for k in range(nz.bit_length() - 1)]
    y_steps = [1 << k for k in range(ny.bit_length() - 1)]
    x_steps = [1 << k for k in range(nx.bit_length() - 1)]

    barrier = pltpu.get_barrier_semaphore()
    greeted = [at_depth(1), twin] + [at_depth(-s) for s in z_steps]
    greeted += [at_plane(-(d // ny), -(d % ny)) for d in range(1, plane)]
    for device in greeted:
        pl.semaphore_signal(barrier, inc=1, device_id=device, device_id_type=MESH)

    mine, key_row = own_keys(rows[...], cols[...])
    left_meta[0] = key_row
    right_meta[0] = key_row
    for t in range(PAIRS):
        pair = jnp.concatenate([values[2 * t], values[2 * t + 1]], axis=1)
        left_panel[t] = pair
        right_panel[t] = pair
    pl.semaphore_wait(barrier, len(greeted))

    def hop(panel, send, recv, way, d, p):
        if way == 0:
            source, target, device = d - 1, d, above
        else:
            source, target, device = lax.rem(nz + 1 - d, nz), nz - d, below
        return pltpu.make_async_remote_copy(
            src_ref=panel.at[pl.ds(source * PAIRS + p, 1)],
            dst_ref=panel.at[pl.ds(target * PAIRS + p, 1)],
            send_sem=send.at[way, d - 1, p],
            recv_sem=recv.at[way, d - 1, p],
            device_id=(me, device),
            device_id_type=MESH,
        )

    far = nz // 2
    split = (PAIRS + 1) // 2

    def last_way(p):
        return 0 if p < split else 1

    def advance(panel, send, recv, d):
        for p in range(PAIRS):
            for way in range(2):
                hop(panel, send, recv, way, d, p).wait_recv()
                hop(panel, send, recv, way, d + 1, p).start()

    def finish(panel, send, recv):
        for p in range(PAIRS):
            for way in range(2):
                hop(panel, send, recv, way, far - 1, p).wait_recv()
                if last_way(p) == way:
                    hop(panel, send, recv, way, far, p).start()
        for p in range(PAIRS):
            hop(panel, send, recv, last_way(p), far, p).wait_recv()

    def settle(panel, send, recv):
        @pl.loop(1, far)
        def _(d):
            for p in range(PAIRS):
                for way in range(2):
                    hop(panel, send, recv, way, d, p).wait_send()

        for p in range(PAIRS):
            hop(panel, send, recv, last_way(p), far, p).wait_send()

    meta_copies = []
    for step in z_steps:
        meta_copies.append((left_meta, step, at_depth(step)))
    for step in y_steps:
        meta_copies.append((right_meta, step, at_plane(0, step)))
    for step in x_steps:
        meta_copies.append((right_meta, step * ny, at_plane(step, 0)))
    meta_copies.append((right_meta, plane, twin))
    meta_copies = [
        pltpu.make_async_remote_copy(
            src_ref=meta.at[pl.ds(0, count)],
            dst_ref=meta.at[pl.ds(count, count)],
            send_sem=meta_send.at[i],
            recv_sem=meta_recv.at[i],
            device_id=device,
            device_id_type=MESH,
        )
        for i, (meta, count, device) in enumerate(meta_copies)
    ]
    meta_left, meta_right = meta_copies[: len(z_steps)], meta_copies[len(z_steps) :]

    def to_plane(d):
        return pltpu.make_async_remote_copy(
            src_ref=right_panel.at[pl.ds(0, PAIRS)],
            dst_ref=right_panel.at[pl.ds(d * PAIRS, PAIRS)],
            send_sem=plane_send.at[d],
            recv_sem=plane_recv.at[d],
            device_id=at_plane(d // ny, lax.rem(d, ny)),
            device_id_type=MESH,
        )

    def to_twin(d):
        return pltpu.make_async_remote_copy(
            src_ref=right_panel.at[pl.ds(d * PAIRS, PAIRS)],
            dst_ref=right_panel.at[pl.ds((plane + d) * PAIRS, PAIRS)],
            send_sem=twin_send.at[d],
            recv_sem=twin_recv.at[d],
            device_id=twin,
            device_id_type=MESH,
        )

    left = (left_panel, left_send, left_recv)
    for p in range(PAIRS):
        for way in range(2):
            hop(*left, way, 1, p).start()
    meta_left[0].start()
    meta_right[0].start()
    to_twin(0).start()

    meta_rounds = max(len(meta_left), len(meta_right))
    for d in range(1, meta_rounds + 1):
        if d < far - 1:
            advance(*left, d)
        for chain in (meta_left, meta_right):
            if d <= len(chain):
                chain[d - 1].wait_recv()
                if d < len(chain):
                    chain[d].start()
        if d < plane:
            to_plane(d).start()
        if 2 < d < plane + 2:
            to_plane(d - 2).wait_recv()
            to_twin(d - 2).start()

    chosen, paired = pair_up(mine, lane_dense(left_meta, nz), lane_dense(right_meta, 2 * plane))
    codes_vector[0:16] = chosen
    codes_vector[16:32] = paired
    codes_copy = pltpu.make_async_copy(codes_vector, codes, codes_sem)
    codes_copy.start()

    next_d = meta_rounds + 1
    both = min(far - 1, plane)
    if next_d < both:
        @pl.loop(next_d, both)
        def _(d):
            advance(*left, d)
            to_plane(d).start()
            to_plane(d - 2).wait_recv()
            to_twin(d - 2).start()

    if max(next_d, both) < far - 1:
        @pl.loop(max(next_d, both), far - 1)
        def _(d):
            advance(*left, d)

    for d in range(max(next_d, both), plane + 2):
        if d < plane:
            to_plane(d).start()
        if 0 < d - 2 < plane:
            to_plane(d - 2).wait_recv()
            to_twin(d - 2).start()

    codes_copy.wait()
    finish(*left)

    @pl.loop(0, plane)
    def _(d):
        to_twin(d).wait_recv()

    second = (square_panel, square_send, square_recv)
    low = lax.broadcasted_iota(jnp.int32, (BLK, LANES), 1) < BLK
    for t in range(PAIRS):
        halves = []
        for half in range(2):
            o = 2 * t + half
            right = right_column(right_panel, codes, o)
            stacked[o] = right
            product = jnp.dot(left_row(left_panel, codes, o), right, preferred_element_type=jnp.float32)
            square[o] = product
            halves.append(product)
        pair = jnp.where(low, halves[0], swap_halves(halves[1]))
        square_panel[t] = pair.astype(square_panel.dtype)
        for way in range(2):
            hop(*second, way, 1, t).start()

    @pl.loop(1, far - 1)
    def _(d):
        advance(*second, d)

    finish(*second)

    for o in range(CAP):
        cube = jnp.dot(left_row(square_panel, codes, o), stacked[o], preferred_element_type=jnp.float32)
        out[o] = (3.0 * square[o] - 2.0 * cube)[:, :BLK]

    settle(*left)
    settle(*second)
    for copy in meta_copies:
        copy.wait_send()

    to_twin(0).wait_send()

    if plane > 1:
        @pl.loop(1, plane)
        def _(d):
            to_plane(d).wait_send()
            to_twin(d).wait_send()


def shards(nx, ny, nz, values, block_rows, block_cols):
    plane = nx * ny
    far = nz // 2
    metas = 2 * 16
    purified = pl.pallas_call(
        functools.partial(kernel, nx, ny, nz),
        out_shape=jax.ShapeDtypeStruct((CAP, BLK, BLK), jnp.float32),
        in_specs=[pl.BlockSpec(memory_space=pltpu.VMEM)] * 3,
        out_specs=pl.BlockSpec(memory_space=pltpu.VMEM),
        scratch_shapes=[
            pltpu.VMEM((nz * PAIRS, BLK, LANES), jnp.bfloat16),
            pltpu.VMEM((2 * plane * PAIRS, BLK, LANES), jnp.bfloat16),
            pltpu.VMEM((nz * PAIRS, BLK, LANES), jnp.bfloat16),
            pltpu.VMEM((CAP, 8 * BLK, LANES), jnp.bfloat16),
            pltpu.VMEM((CAP, BLK, LANES), jnp.float32),
            pltpu.VMEM((nz, 1, LANES), jnp.int32),
            pltpu.VMEM((2 * plane, 1, LANES), jnp.int32),
            pltpu.VMEM((32, LANES), jnp.int32),
            pltpu.SMEM((32, LANES), jnp.int32),
            pltpu.SemaphoreType.DMA((2, far, PAIRS)),
            pltpu.SemaphoreType.DMA((2, far, PAIRS)),
            pltpu.SemaphoreType.DMA((2, far, PAIRS)),
            pltpu.SemaphoreType.DMA((2, far, PAIRS)),
            pltpu.SemaphoreType.DMA((plane,)),
            pltpu.SemaphoreType.DMA((plane,)),
            pltpu.SemaphoreType.DMA((plane,)),
            pltpu.SemaphoreType.DMA((plane,)),
            pltpu.SemaphoreType.DMA((metas,)),
            pltpu.SemaphoreType.DMA((metas,)),
            pltpu.SemaphoreType.DMA,
        ],
        compiler_params=pltpu.CompilerParams(
            collective_id=0, has_side_effects=True, vmem_limit_bytes=40 * 1024 * 1024
        ),
    )(values.reshape(values.shape[2:]), block_rows.reshape(1, CAP), block_cols.reshape(1, CAP))
    return purified.reshape(values.shape)


PLANES = {32: (4, 4), 8: (2, 2), 2: (1, 1)}


def solution(mesh):
    nx, ny = PLANES[mesh.shape["row"]]
    body = functools.partial(shards, nx, ny, mesh.shape["col"])
    in_specs = (P("row", "col", None, None, None), P("row", "col", None), P("row", "col", None))
    out_specs = P("row", "col", None, None, None)
    return jax.shard_map(body, mesh=mesh, in_specs=in_specs, out_specs=out_specs, check_vma=False)
```

time: 407 us -> 160 us (0.39)
  the two profiles are of different devices: /device:TPU:12 before, /device:TPU:8 now
where the time goes in v1:
time: 160 us
  Pallas kernels  158 us (99%)
  local copies, waits for them, and re-layouts  2.31 us (1%)
    pallas_call x1, Pallas kernels, shards(): pl.pallas_call(functools.partial(kernel, nx, ny, nz), out_shape=jax.Shape...  158 us

profile of v1, /device:TPU:8, one launch (start us, length us, event | category | flops | bytes accessed | tf_op | source)
XLA Modules:
  0.0 160.0 jit_solution(3877791583494554153)
XLA Ops:
  0.0 0.0 copy-start.1
  0.0 0.0 copy-start.2
  0.0 0.7 copy-done.1
  0.7 0.0 copy-done.2
  0.7 0.0 copy-start
  0.7 0.9 copy-done
  1.6 157.7 %shard_map.37 = f32[10,64,64]{2,1,0:T(8,128)S(1)} custom-call(bf16[10,64,64]{2,1,0:T(8,128)(2,1)S(1)} %bitcast.5, s32[1,10]{1,0:T(1,128)S(1)} %bitcast.6, s32[1,10]{1,0:T(1,128)S(1)} %bitcast.7), custom_call_target="tpu_custom_call" | custom-call | tf_op jit(solution)/shard_map/pallas_call | solution.py:329
  159.2 0.7 copy.5
Async XLA Ops:
  0.0 0.7 copy-start.1
  0.0 0.7 copy-start.2
  0.7 0.9 copy-start

commit v2 on v1

--- a/solution.py
+++ b/solution.py
@@ -11,6 +11,7 @@
 CAP = 10
 BLK = 64
 PAIRS = CAP // 2
+PIECES = ((0, 3), (3, 2))
 LANES = 128
 SHIFT = 11
 BIG = 1 << 30
@@ -110,7 +111,6 @@
     me, z = lax.axis_index("row"), lax.axis_index("col")
     core = lax.rem(me, 2)
     x, y = me // (2 * ny), lax.rem(me // 2, ny)
-    above, below = lax.rem(z + 1, nz), lax.rem(z + nz - 1, nz)
     twin = (me + 1 - 2 * core, z)
 
     def at_plane(dx, dy):
@@ -124,7 +124,7 @@
     x_steps = [1 << k for k in range(nx.bit_length() - 1)]
 
     barrier = pltpu.get_barrier_semaphore()
-    greeted = [at_depth(1), twin] + [at_depth(-s) for s in z_steps]
+    greeted = [at_depth(1), at_depth(2), twin] + [at_depth(-s) for s in z_steps]
     greeted += [at_plane(-(d // ny), -(d % ny)) for d in range(1, plane)]
     for device in greeted:
         pl.semaphore_signal(barrier, inc=1, device_id=device, device_id_type=MESH)
@@ -138,60 +138,64 @@
         right_panel[t] = pair
     pl.semaphore_wait(barrier, len(greeted))
 
-    def hop(panel, send, recv, way, d, p):
+    far = nz // 2
+    stages = far // 2
+
+    def hop(ring, way, source, target, p):
+        panel, send, recv = ring
+        first, count = PIECES[p]
+        gap = target - source
         if way == 0:
-            source, target, device = d - 1, d, above
+            here, there = source, target
         else:
-            source, target, device = lax.rem(nz + 1 - d, nz), nz - d, below
+            here, there, gap = lax.rem(nz - source, nz), nz - target, -gap
         return pltpu.make_async_remote_copy(
-            src_ref=panel.at[pl.ds(source * PAIRS + p, 1)],
-            dst_ref=panel.at[pl.ds(target * PAIRS + p, 1)],
-            send_sem=send.at[way, d - 1, p],
-            recv_sem=recv.at[way, d - 1, p],
-            device_id=(me, device),
+            src_ref=panel.at[pl.ds(here * PAIRS + first, count)],
+            dst_ref=panel.at[pl.ds(there * PAIRS + first, count)],
+            send_sem=send.at[way, target - 1, p],
+            recv_sem=recv.at[way, target - 1, p],
+            device_id=at_depth(gap),
             device_id_type=MESH,
         )
 
-    far = nz // 2
-    split = (PAIRS + 1) // 2
-
-    def last_way(p):
-        return 0 if p < split else 1
-
-    def advance(panel, send, recv, d):
-        for p in range(PAIRS):
-            for way in range(2):
-                hop(panel, send, recv, way, d, p).wait_recv()
-                hop(panel, send, recv, way, d + 1, p).start()
-
-    def finish(panel, send, recv):
-        for p in range(PAIRS):
-            for way in range(2):
-                hop(panel, send, recv, way, far - 1, p).wait_recv()
-                if last_way(p) == way:
-                    hop(panel, send, recv, way, far, p).start()
-        for p in range(PAIRS):
-            hop(panel, send, recv, last_way(p), far, p).wait_recv()
-
-    def settle(panel, send, recv):
-        @pl.loop(1, far)
-        def _(d):
-            for p in range(PAIRS):
-                for way in range(2):
-                    hop(panel, send, recv, way, d, p).wait_send()
-
-        for p in range(PAIRS):
-            hop(panel, send, recv, last_way(p), far, p).wait_send()
-
-    meta_copies = []
-    for step in z_steps:
-        meta_copies.append((left_meta, step, at_depth(step)))
-    for step in y_steps:
-        meta_copies.append((right_meta, step, at_plane(0, step)))
-    for step in x_steps:
-        meta_copies.append((right_meta, step * ny, at_plane(step, 0)))
-    meta_copies.append((right_meta, plane, twin))
-    meta_copies = [
+    lanes_of = [(p, way) for p in range(len(PIECES)) for way in range(2)]
+
+    def stage(ring, k, p, way, wait=True, last=False):
+        base = 2 * k - 2
+        if wait:
+            hop(ring, way, base - 2, base, p).wait_recv()
+        if not last or way == p % 2:
+            hop(ring, way, base, base + 2, p).start()
+        hop(ring, way, base, base + 1, p).start()
+
+    def arrive(ring):
+        @pl.loop(1, stages + 1)
+        def _(k):
+            for p, way in lanes_of:
+                hop(ring, way, 2 * k - 2, 2 * k - 1, p).wait_recv()
+
+        for p in range(len(PIECES)):
+            hop(ring, p % 2, far - 2, far, p).wait_recv()
+
+    def settle(ring):
+        @pl.loop(1, stages + 1)
+        def _(k):
+            for p, way in lanes_of:
+                hop(ring, way, 2 * k - 2, 2 * k - 1, p).wait_send()
+
+        @pl.loop(1, stages)
+        def _(k):
+            for p, way in lanes_of:
+                hop(ring, way, 2 * k - 2, 2 * k, p).wait_send()
+
+        for p in range(len(PIECES)):
+            hop(ring, p % 2, far - 2, far, p).wait_send()
+
+    metas = [(left_meta, step, at_depth(step)) for step in z_steps]
+    metas += [(right_meta, step, at_plane(0, step)) for step in y_steps]
+    metas += [(right_meta, step * ny, at_plane(step, 0)) for step in x_steps]
+    metas += [(right_meta, plane, twin)]
+    metas = [
         pltpu.make_async_remote_copy(
             src_ref=meta.at[pl.ds(0, count)],
             dst_ref=meta.at[pl.ds(count, count)],
@@ -200,9 +204,10 @@
             device_id=device,
             device_id_type=MESH,
         )
-        for i, (meta, count, device) in enumerate(meta_copies)
+        for i, (meta, count, device) in enumerate(metas)
     ]
-    meta_left, meta_right = meta_copies[: len(z_steps)], meta_copies[len(z_steps) :]
+    chains = [metas[: len(z_steps)], metas[len(z_steps) :]]
+    rounds = max(len(chain) for chain in chains)
 
     def to_plane(d):
         return pltpu.make_async_remote_copy(
@@ -224,93 +229,84 @@
             device_id_type=MESH,
         )
 
-    left = (left_panel, left_send, left_recv)
-    for p in range(PAIRS):
-        for way in range(2):
-            hop(*left, way, 1, p).start()
-    meta_left[0].start()
-    meta_right[0].start()
-    to_twin(0).start()
-
-    meta_rounds = max(len(meta_left), len(meta_right))
-    for d in range(1, meta_rounds + 1):
-        if d < far - 1:
-            advance(*left, d)
-        for chain in (meta_left, meta_right):
-            if d <= len(chain):
-                chain[d - 1].wait_recv()
-                if d < len(chain):
-                    chain[d].start()
-        if d < plane:
+    group = -(-(plane - 1) // rounds)
+
+    def beside(k):
+        for chain in chains:
+            if 0 < k <= len(chain):
+                chain[k - 1].wait_recv()
+            if k < len(chain):
+                chain[k].start()
+        if k == 0:
+            to_twin(0).start()
+        for d in range(1 + (k - 1) * group, min(plane, 1 + k * group)):
+            if d > 0:
+                to_plane(d).wait_recv()
+                to_twin(d).start()
+        for d in range(1 + k * group, min(plane, 1 + (k + 1) * group)):
             to_plane(d).start()
-        if 2 < d < plane + 2:
-            to_plane(d - 2).wait_recv()
-            to_twin(d - 2).start()
-
-    chosen, paired = pair_up(mine, lane_dense(left_meta, nz), lane_dense(right_meta, 2 * plane))
-    codes_vector[0:16] = chosen
-    codes_vector[16:32] = paired
+        if k == rounds:
+            chosen, paired = pair_up(mine, lane_dense(left_meta, nz), lane_dense(right_meta, 2 * plane))
+            codes_vector[0:16] = chosen
+            codes_vector[16:32] = paired
+            codes_copy.start()
+        if k == rounds + 2:
+            codes_copy.wait()
+
+            @pl.loop(0, plane)
+            def _(d):
+                to_twin(d).wait_recv()
+
+            @pl.loop(0, CAP)
+            def _(o):
+                stacked[o] = right_column(right_panel, codes, o)
+
     codes_copy = pltpu.make_async_copy(codes_vector, codes, codes_sem)
-    codes_copy.start()
-
-    next_d = meta_rounds + 1
-    both = min(far - 1, plane)
-    if next_d < both:
-        @pl.loop(next_d, both)
-        def _(d):
-            advance(*left, d)
-            to_plane(d).start()
-            to_plane(d - 2).wait_recv()
-            to_twin(d - 2).start()
-
-    if max(next_d, both) < far - 1:
-        @pl.loop(max(next_d, both), far - 1)
-        def _(d):
-            advance(*left, d)
-
-    for d in range(max(next_d, both), plane + 2):
-        if d < plane:
-            to_plane(d).start()
-        if 0 < d - 2 < plane:
-            to_plane(d - 2).wait_recv()
-            to_twin(d - 2).start()
-
-    codes_copy.wait()
-    finish(*left)
-
-    @pl.loop(0, plane)
-    def _(d):
-        to_twin(d).wait_recv()
+    first = (left_panel, left_send, left_recv)
+    for k in range(max(stages, rounds + 3)):
+        if k < stages:
+            for p, way in lanes_of:
+                stage(first, k + 1, p, way, wait=k > 0, last=k == stages - 1)
+        beside(k)
+    arrive(first)
 
     second = (square_panel, square_send, square_recv)
     low = lax.broadcasted_iota(jnp.int32, (BLK, LANES), 1) < BLK
-    for t in range(PAIRS):
+
+    def square_pair(t):
         halves = []
         for half in range(2):
             o = 2 * t + half
-            right = right_column(right_panel, codes, o)
-            stacked[o] = right
-            product = jnp.dot(left_row(left_panel, codes, o), right, preferred_element_type=jnp.float32)
+            product = jnp.dot(left_row(left_panel, codes, o), stacked[o], preferred_element_type=jnp.float32)
             square[o] = product
             halves.append(product)
         pair = jnp.where(low, halves[0], swap_halves(halves[1]))
         square_panel[t] = pair.astype(square_panel.dtype)
+
+    for p, (start, count) in enumerate(PIECES):
+        pl.loop(start, start + count)(square_pair)
         for way in range(2):
-            hop(*second, way, 1, t).start()
-
-    @pl.loop(1, far - 1)
-    def _(d):
-        advance(*second, d)
-
-    finish(*second)
-
-    for o in range(CAP):
+            stage(second, 1, p, way, wait=False, last=stages == 1)
+
+    if stages > 2:
+        @pl.loop(2, stages)
+        def _(k):
+            for p, way in lanes_of:
+                stage(second, k, p, way)
+
+    if stages > 1:
+        for p, way in lanes_of:
+            stage(second, stages, p, way, last=True)
+    arrive(second)
+
+    @pl.loop(0, CAP)
+    def _(o):
         cube = jnp.dot(left_row(square_panel, codes, o), stacked[o], preferred_element_type=jnp.float32)
         out[o] = (3.0 * square[o] - 2.0 * cube)[:, :BLK]
 
-    settle(*left)
-    settle(*second)
-    for copy in meta_copies:
+    settle(first)
+    settle(second)
+    for copy in metas:
         copy.wait_send()
 
     to_twin(0).wait_send()
@@ -341,10 +337,10 @@
             pltpu.VMEM((2 * plane, 1, LANES), jnp.int32),
             pltpu.VMEM((32, LANES), jnp.int32),
             pltpu.SMEM((32, LANES), jnp.int32),
-            pltpu.SemaphoreType.DMA((2, far, PAIRS)),
-            pltpu.SemaphoreType.DMA((2, far, PAIRS)),
-            pltpu.SemaphoreType.DMA((2, far, PAIRS)),
-            pltpu.SemaphoreType.DMA((2, far, PAIRS)),
+            pltpu.SemaphoreType.DMA((2, far, len(PIECES))),
+            pltpu.SemaphoreType.DMA((2, far, len(PIECES))),
+            pltpu.SemaphoreType.DMA((2, far, len(PIECES))),
+            pltpu.SemaphoreType.DMA((2, far, len(PIECES))),
             pltpu.SemaphoreType.DMA((plane,)),
             pltpu.SemaphoreType.DMA((plane,)),
             pltpu.SemaphoreType.DMA((plane,)),

time: 160 us -> 133 us (0.83)
  the two profiles are of different devices: /device:TPU:8 before, /device:TPU:28 now
where the time goes in v2:
time: 133 us
  Pallas kernels  131 us (98%)
  local copies, waits for them, and re-layouts  2.31 us (2%)
    pallas_call x1, Pallas kernels, shards(): pl.pallas_call(functools.partial(kernel, nx, ny, nz), out_shape=jax.Shape...  131 us

profile of v2, /device:TPU:28, one launch (start us, length us, event | category | flops | bytes accessed | tf_op | source)
XLA Modules:
  0.0 132.8 jit_solution(5487969342525907685)
XLA Ops:
  0.0 0.0 copy-start.1
  0.0 0.0 copy-start.2
  0.0 0.7 copy-done.1
  0.7 0.0 copy-done.2
  0.7 0.0 copy-start
  0.7 0.9 copy-done
  1.6 130.5 %shard_map.37 = f32[10,64,64]{2,1,0:T(8,128)S(1)} custom-call(bf16[10,64,64]{2,1,0:T(8,128)(2,1)S(1)} %bitcast.5, s32[1,10]{1,0:T(1,128)S(1)} %bitcast.6, s32[1,10]{1,0:T(1,128)S(1)} %bitcast.7), custom_call_target="tpu_custom_call" | custom-call | tf_op jit(solution)/shard_map/pallas_call | solution.py:325
  132.1 0.7 copy.5
Async XLA Ops:
  0.0 0.7 copy-start.1
  0.0 0.7 copy-start.2
  0.7 0.9 copy-start

commit v3 on v2

--- a/solution.py
+++ b/solution.py
@@ -12,6 +12,7 @@
 BLK = 64
 PAIRS = CAP // 2
 PIECES = ((0, 3), (3, 2))
+KEYS = len(PIECES)
 LANES = 128
 SHIFT = 11
 BIG = 1 << 30
@@ -119,12 +120,11 @@
     def at_depth(dz):
         return me, lax.rem(z + dz + nz, nz)
 
-    z_steps = [1 << k for k in range(nz.bit_length() - 1)]
     y_steps = [1 << k for k in range(ny.bit_length() - 1)]
     x_steps = [1 << k for k in range(nx.bit_length() - 1)]
 
     barrier = pltpu.get_barrier_semaphore()
-    greeted = [at_depth(1), at_depth(2), twin] + [at_depth(-s) for s in z_steps]
+    greeted = [twin] + [at_depth(s) for s in (1, 2, -1, -2)]
     greeted += [at_plane(-(d // ny), -(d % ny)) for d in range(1, plane)]
     for device in greeted:
         pl.semaphore_signal(barrier, inc=1, device_id=device, device_id_type=MESH)
@@ -142,57 +142,66 @@
     stages = far // 2
 
     def hop(ring, way, source, target, p):
-        panel, send, recv = ring
-        first, count = PIECES[p]
+        panel, keys, send, recv = ring
         gap = target - source
         if way == 0:
             here, there = source, target
         else:
             here, there, gap = lax.rem(nz - source, nz), nz - target, -gap
+        if p == KEYS:
+            src, dst = keys.at[pl.ds(here, 1)], keys.at[pl.ds(there, 1)]
+        else:
+            first, count = PIECES[p]
+            src, dst = panel.at[pl.ds(here * PAIRS + first, count)], panel.at[pl.ds(there * PAIRS + first, count)]
         return pltpu.make_async_remote_copy(
-            src_ref=panel.at[pl.ds(here * PAIRS + first, count)],
-            dst_ref=panel.at[pl.ds(there * PAIRS + first, count)],
+            src_ref=src,
+            dst_ref=dst,
             send_sem=send.at[way, target - 1, p],
             recv_sem=recv.at[way, target - 1, p],
             device_id=at_depth(gap),
             device_id_type=MESH,
         )
 
-    lanes_of = [(p, way) for p in range(len(PIECES)) for way in range(2)]
+    pieces = tuple(range(len(PIECES)))
+
+    def last_way(p):
+        return 1 if p == 1 else 0
 
     def stage(ring, k, p, way, wait=True, last=False):
         base = 2 * k - 2
         if wait:
             hop(ring, way, base - 2, base, p).wait_recv()
-        if not last or way == p % 2:
+        if not last or way == last_way(p):
             hop(ring, way, base, base + 2, p).start()
         hop(ring, way, base, base + 1, p).start()
 
-    def arrive(ring):
+    def arrive(ring, parts):
         @pl.loop(1, stages + 1)
         def _(k):
-            for p, way in lanes_of:
-                hop(ring, way, 2 * k - 2, 2 * k - 1, p).wait_recv()
-
-        for p in range(len(PIECES)):
-            hop(ring, p % 2, far - 2, far, p).wait_recv()
-
-    def settle(ring):
+            for p in parts:
+                for way in range(2):
+                    hop(ring, way, 2 * k - 2, 2 * k - 1, p).wait_recv()
+
+        for p in parts:
+            hop(ring, last_way(p), far - 2, far, p).wait_recv()
+
+    def settle(ring, parts):
         @pl.loop(1, stages + 1)
         def _(k):
-            for p, way in lanes_of:
-                hop(ring, way, 2 * k - 2, 2 * k - 1, p).wait_send()
+            for p in parts:
+                for way in range(2):
+                    hop(ring, way, 2 * k - 2, 2 * k - 1, p).wait_send()
 
         @pl.loop(1, stages)
         def _(k):
-            for p, way in lanes_of:
-                hop(ring, way, 2 * k - 2, 2 * k, p).wait_send()
-
-        for p in range(len(PIECES)):
-            hop(ring, p % 2, far - 2, far, p).wait_send()
-
-    metas = [(left_meta, step, at_depth(step)) for step in z_steps]
-    metas += [(right_meta, step, at_plane(0, step)) for step in y_steps]
+            for p in parts:
+                for way in range(2):
+                    hop(ring, way, 2 * k - 2, 2 * k, p).wait_send()
+
+        for p in parts:
+            hop(ring, last_way(p), far - 2, far, p).wait_send()
+
+    metas = [(right_meta, step, at_plane(0, step)) for step in y_steps]
     metas += [(right_meta, step * ny, at_plane(step, 0)) for step in x_steps]
     metas += [(right_meta, plane, twin)]
     metas = [
@@ -206,8 +215,7 @@
         )
         for i, (meta, count, device) in enumerate(metas)
     ]
-    chains = [metas[: len(z_steps)], metas[len(z_steps) :]]
-    rounds = max(len(chain) for chain in chains)
+    rounds = len(metas)
 
     def to_plane(d):
         return pltpu.make_async_remote_copy(
@@ -232,11 +240,10 @@
     group = -(-(plane - 1) // rounds)
 
     def beside(k):
-        for chain in chains:
-            if 0 < k <= len(chain):
-                chain[k - 1].wait_recv()
-            if k < len(chain):
-                chain[k].start()
+        if 0 < k <= rounds:
+            metas[k - 1].wait_recv()
+        if k < rounds:
+            metas[k].start()
         if k == 0:
             to_twin(0).start()
         for d in range(1 + (k - 1) * group, min(plane, 1 + k * group)):
@@ -245,32 +252,35 @@
                 to_twin(d).start()
         for d in range(1 + k * group, min(plane, 1 + (k + 1) * group)):
             to_plane(d).start()
-        if k == rounds:
-            chosen, paired = pair_up(mine, lane_dense(left_meta, nz), lane_dense(right_meta, 2 * plane))
-            codes_vector[0:16] = chosen
-            codes_vector[16:32] = paired
-            codes_copy.start()
-        if k == rounds + 2:
-            codes_copy.wait()
-
-            @pl.loop(0, plane)
-            def _(d):
-                to_twin(d).wait_recv()
-
-            @pl.loop(0, CAP)
-            def _(o):
-                stacked[o] = right_column(right_panel, codes, o)
 
     codes_copy = pltpu.make_async_copy(codes_vector, codes, codes_sem)
-    first = (left_panel, left_send, left_recv)
-    for k in range(max(stages, rounds + 3)):
+    first = (left_panel, left_meta, left_send, left_recv)
+    for k in range(max(stages, rounds + 1)):
         if k < stages:
-            for p, way in lanes_of:
-                stage(first, k + 1, p, way, wait=k > 0, last=k == stages - 1)
+            for p in (KEYS,) + pieces:
+                for way in range(2):
+                    stage(first, k + 1, p, way, wait=k > 0, last=k == stages - 1)
         beside(k)
-    arrive(first)
-
-    second = (square_panel, square_send, square_recv)
+
+    arrive(first, (KEYS,))
+    chosen, paired = pair_up(mine, lane_dense(left_meta, nz), lane_dense(right_meta, 2 * plane))
+    codes_vector[0:16] = chosen
+    codes_vector[16:32] = paired
+    codes_copy.start()
+
+    @pl.loop(0, plane)
+    def _(d):
+        to_twin(d).wait_recv()
+
+    codes_copy.wait()
+
+    @pl.loop(0, CAP)
+    def _(o):
+        stacked[o] = right_column(right_panel, codes, o)
+
+    arrive(first, pieces)
+
+    second = (square_panel, None, square_send, square_recv)
     low = lax.broadcasted_iota(jnp.int32, (BLK, LANES), 1) < BLK
 
     def square_pair(t):
@@ -291,21 +301,23 @@
     if stages > 2:
         @pl.loop(2, stages)
         def _(k):
-            for p, way in lanes_of:
-                stage(second, k, p, way)
+            for p in pieces:
+                for way in range(2):
+                    stage(second, k, p, way)
 
     if stages > 1:
-        for p, way in lanes_of:
-            stage(second, stages, p, way, last=True)
-    arrive(second)
+        for p in pieces:
+            for way in range(2):
+                stage(second, stages, p, way, last=True)
+    arrive(second, pieces)
 
     @pl.loop(0, CAP)
     def _(o):
         cube = jnp.dot(left_row(square_panel, codes, o), stacked[o], preferred_element_type=jnp.float32)
         out[o] = (3.0 * square[o] - 2.0 * cube)[:, :BLK]
 
-    settle(first)
-    settle(second)
+    settle(first, (KEYS,) + pieces)
+    settle(second, pieces)
     for copy in metas:
         copy.wait_send()
 
@@ -337,8 +349,8 @@
             pltpu.VMEM((2 * plane, 1, LANES), jnp.int32),
             pltpu.VMEM((32, LANES), jnp.int32),
             pltpu.SMEM((32, LANES), jnp.int32),
-            pltpu.SemaphoreType.DMA((2, far, len(PIECES))),
-            pltpu.SemaphoreType.DMA((2, far, len(PIECES))),
+            pltpu.SemaphoreType.DMA((2, far, len(PIECES) + 1)),
+            pltpu.SemaphoreType.DMA((2, far, len(PIECES) + 1)),
             pltpu.SemaphoreType.DMA((2, far, len(PIECES))),
             pltpu.SemaphoreType.DMA((2, far, len(PIECES))),
             pltpu.SemaphoreType.DMA((plane,)),

time: 133 us -> 121 us (0.910)
  the two profiles are of different devices: /device:TPU:28 before, /device:TPU:32 now
where the time goes in v3:
time: 121 us; the launch traced here: 120 us
  Pallas kernels  118 us (98%)
  local copies, waits for them, and re-layouts  2.31 us (2%)
    pallas_call x1, Pallas kernels, shards(): pl.pallas_call(functools.partial(kernel, nx, ny, nz), out_shape=jax.Shape...  118 us

profile of v3, /device:TPU:32, one launch (start us, length us, event | category | flops | bytes accessed | tf_op | source)
XLA Modules:
  0.0 120.5 jit_solution(6743562101634025880)
XLA Ops:
  0.0 0.0 copy-start.1
  0.0 0.0 copy-start.2
  0.0 0.7 copy-done.1
  0.7 0.0 copy-done.2
  0.7 0.0 copy-start
  0.7 0.9 copy-done
  1.6 118.2 %shard_map.37 = f32[10,64,64]{2,1,0:T(8,128)S(1)} custom-call(bf16[10,64,64]{2,1,0:T(8,128)(2,1)S(1)} %bitcast.5, s32[1,10]{1,0:T(1,128)S(1)} %bitcast.6, s32[1,10]{1,0:T(1,128)S(1)} %bitcast.7), custom_call_target="tpu_custom_call" | custom-call | tf_op jit(solution)/shard_map/pallas_call | solution.py:337
  119.8 0.7 copy.5
Async XLA Ops:
  0.0 0.7 copy-start.1
  0.0 0.7 copy-start.2
  0.7 0.9 copy-start

commit v4 on v3

--- a/solution.py
+++ b/solution.py
@@ -101,7 +101,8 @@
 
 def kernel(
     nx, ny, nz,
-    values, rows, cols, out,
+    values_hbm, rows_hbm, cols_hbm, out,
+    values, rows, cols, in_sem,
     left_panel, right_panel, square_panel, stacked, square,
     left_meta, right_meta, codes_vector, codes,
     left_send, left_recv, square_send, square_recv,
@@ -123,12 +124,21 @@
     y_steps = [1 << k for k in range(ny.bit_length() - 1)]
     x_steps = [1 << k for k in range(nx.bit_length() - 1)]
 
+    reads = [
+        pltpu.make_async_copy(source, target, in_sem.at[i])
+        for i, (source, target) in enumerate(((rows_hbm, rows), (cols_hbm, cols), (values_hbm, values)))
+    ]
+    for read in reads:
+        read.start()
+
     barrier = pltpu.get_barrier_semaphore()
     greeted = [twin] + [at_depth(s) for s in (1, 2, -1, -2)]
     greeted += [at_plane(-(d // ny), -(d % ny)) for d in range(1, plane)]
     for device in greeted:
         pl.semaphore_signal(barrier, inc=1, device_id=device, device_id_type=MESH)
 
+    for read in reads:
+        read.wait()
     mine, key_row = own_keys(rows[...], cols[...])
     left_meta[0] = key_row
     right_meta[0] = key_row
@@ -140,6 +150,7 @@
 
     far = nz // 2
     stages = far // 2
+    depth = {gap: at_depth(gap) for gap in (1, 2, -1, -2)}
 
     def hop(ring, way, source, target, p):
         panel, keys, send, recv = ring
@@ -147,7 +158,7 @@
         if way == 0:
             here, there = source, target
         else:
-            here, there, gap = lax.rem(nz - source, nz), nz - target, -gap
+            here, there, gap = (nz - source) % nz, nz - target, -gap
         if p == KEYS:
             src, dst = keys.at[pl.ds(here, 1)], keys.at[pl.ds(there, 1)]
         else:
@@ -158,7 +169,7 @@
             dst_ref=dst,
             send_sem=send.at[way, target - 1, p],
             recv_sem=recv.at[way, target - 1, p],
-            device_id=at_depth(gap),
+            device_id=depth[gap],
             device_id_type=MESH,
         )
 
@@ -167,39 +178,30 @@
     def last_way(p):
         return 1 if p == 1 else 0
 
-    def stage(ring, k, p, way, wait=True, last=False):
-        base = 2 * k - 2
-        if wait:
+    def stage(ring, k, p, way):
+        base, last = 2 * k - 2, k == stages
+        if k > 1:
             hop(ring, way, base - 2, base, p).wait_recv()
         if not last or way == last_way(p):
             hop(ring, way, base, base + 2, p).start()
         hop(ring, way, base, base + 1, p).start()
 
-    def arrive(ring, parts):
-        @pl.loop(1, stages + 1)
-        def _(k):
-            for p in parts:
-                for way in range(2):
-                    hop(ring, way, 2 * k - 2, 2 * k - 1, p).wait_recv()
-
+    def between_in(ring, k, parts):
+        for p in parts:
+            for way in range(2):
+                hop(ring, way, 2 * k - 2, 2 * k - 1, p).wait_recv()
+
+    def sent(ring, k, parts):
+        for p in parts:
+            for way in range(2):
+                hop(ring, way, 2 * k - 2, 2 * k - 1, p).wait_send()
+                if k < stages or way == last_way(p):
+                    hop(ring, way, 2 * k - 2, 2 * k, p).wait_send()
+
+    def last_in(ring, parts):
         for p in parts:
             hop(ring, last_way(p), far - 2, far, p).wait_recv()
-
-    def settle(ring, parts):
-        @pl.loop(1, stages + 1)
-        def _(k):
-            for p in parts:
-                for way in range(2):
-                    hop(ring, way, 2 * k - 2, 2 * k - 1, p).wait_send()
-
-        @pl.loop(1, stages)
-        def _(k):
-            for p in parts:
-                for way in range(2):
-                    hop(ring, way, 2 * k - 2, 2 * k, p).wait_send()
-
-        for p in parts:
-            hop(ring, last_way(p), far - 2, far, p).wait_send()
+        between_in(ring, stages, parts)
 
     metas = [(right_meta, step, at_plane(0, step)) for step in y_steps]
     metas += [(right_meta, step * ny, at_plane(step, 0)) for step in x_steps]
@@ -259,10 +261,12 @@
         if k < stages:
             for p in (KEYS,) + pieces:
                 for way in range(2):
-                    stage(first, k + 1, p, way, wait=k > 0, last=k == stages - 1)
+                    stage(first, k + 1, p, way)
         beside(k)
-
-    arrive(first, (KEYS,))
+        if 0 < k < stages:
+            between_in(first, k, (KEYS,) + pieces)
+
+    last_in(first, (KEYS,))
     chosen, paired = pair_up(mine, lane_dense(left_meta, nz), lane_dense(right_meta, 2 * plane))
     codes_vector[0:16] = chosen
     codes_vector[16:32] = paired
@@ -278,7 +282,7 @@
     def _(o):
         stacked[o] = right_column(right_panel, codes, o)
 
-    arrive(first, pieces)
+    last_in(first, pieces)
 
     second = (square_panel, None, square_send, square_recv)
     low = lax.broadcasted_iota(jnp.int32, (BLK, LANES), 1) < BLK
@@ -296,38 +300,26 @@
     for p, (start, count) in enumerate(PIECES):
         pl.loop(start, start + count)(square_pair)
         for way in range(2):
-            stage(second, 1, p, way, wait=False, last=stages == 1)
-
-    if stages > 2:
-        @pl.loop(2, stages)
-        def _(k):
+            stage(second, 1, p, way)
+
+    for k in range(1, stages + 1):
+        if k > 1:
             for p in pieces:
                 for way in range(2):
                     stage(second, k, p, way)
-
-    if stages > 1:
-        for p in pieces:
-            for way in range(2):
-                stage(second, stages, p, way, last=True)
-    arrive(second, pieces)
+            between_in(second, k - 1, pieces)
+            sent(second, k - 1, pieces)
+        sent(first, k, (KEYS,) + pieces)
+        for copy in (metas + [to_twin(d) for d in range(plane)] + [to_plane(d) for d in range(1, plane)])[k - 1 :: stages]:
+            copy.wait_send()
+    last_in(second, pieces)
 
     @pl.loop(0, CAP)
     def _(o):
         cube = jnp.dot(left_row(square_panel, codes, o), stacked[o], preferred_element_type=jnp.float32)
         out[o] = (3.0 * square[o] - 2.0 * cube)[:, :BLK]
 
-    settle(first, (KEYS,) + pieces)
-    settle(second, pieces)
-    for copy in metas:
-        copy.wait_send()
-
-    to_twin(0).wait_send()
-
-    if plane > 1:
-        @pl.loop(1, plane)
-        def _(d):
-            to_plane(d).wait_send()
-            to_twin(d).wait_send()
+    sent(second, stages, pieces)
 
 
 def shards(nx, ny, nz, values, block_rows, block_cols):
@@ -337,9 +329,13 @@
     purified = pl.pallas_call(
         functools.partial(kernel, nx, ny, nz),
         out_shape=jax.ShapeDtypeStruct((CAP, BLK, BLK), jnp.float32),
-        in_specs=[pl.BlockSpec(memory_space=pltpu.VMEM)] * 3,
+        in_specs=[pl.BlockSpec(memory_space=pl.ANY)] * 3,
         out_specs=pl.BlockSpec(memory_space=pltpu.VMEM),
         scratch_shapes=[
+            pltpu.VMEM((CAP, BLK, BLK), jnp.bfloat16),
+            pltpu.VMEM((1, CAP), jnp.int32),
+            pltpu.VMEM((1, CAP), jnp.int32),
+            pltpu.SemaphoreType.DMA((3,)),
             pltpu.VMEM((nz * PAIRS, BLK, LANES), jnp.bfloat16),
             pltpu.VMEM((2 * plane * PAIRS, BLK, LANES), jnp.bfloat16),
             pltpu.VMEM((nz * PAIRS, BLK, LANES), jnp.bfloat16),
@@ -362,7 +358,7 @@
             pltpu.SemaphoreType.DMA,
         ],
         compiler_params=pltpu.CompilerParams(
-            collective_id=0, has_side_effects=True, vmem_limit_bytes=40 * 1024 * 1024
+            collective_id=0, has_side_effects=True, vmem_limit_bytes=60 * 1024 * 1024
         ),
     )(values.reshape(values.shape[2:]), block_rows.reshape(1, CAP), block_cols.reshape(1, CAP))
     return purified.reshape(values.shape)

time: 121 us -> 120 us (level)
  no operation moved by 1% of the time
where the time goes in v4:
time: 120 us
  Pallas kernels  118 us (98%)
  local copies, waits for them, and re-layouts  1.72 us (1%)
    pallas_call x1, Pallas kernels, shards(): pl.pallas_call(functools.partial(kernel, nx, ny, nz), out_shape=jax.Shape...  118 us

profile of v4, /device:TPU:32, one launch (start us, length us, event | category | flops | bytes accessed | tf_op | source)
XLA Modules:
  0.0 120.2 jit_solution(522502348468971670)
XLA Ops:
  0.0 118.5 %shard_map.37 = f32[10,64,64]{2,1,0:T(8,128)} custom-call(bf16[10,64,64]{2,1,0:T(8,128)(2,1)} %bitcast.5, s32[1,10]{1,0:T(1,128)} %bitcast.6, s32[1,10]{1,0:T(1,128)} %bitcast.7), custom_call_target="tpu_custom_call" | custom-call | tf_op jit(solution)/shard_map/pallas_call | solution.py:329
  118.5 1.7 %copy.5 = f32[1,1,10,64,64]{4,3,2,1,0:T(8,128)} copy(f32[1,1,10,64,64]{4,3,2,1,0:T(8,128)} %bitcast.4) | data formatting | bytes 327680

commit v5 on v4

--- a/solution.py
+++ b/solution.py
@@ -133,7 +133,7 @@
 
     barrier = pltpu.get_barrier_semaphore()
     greeted = [twin] + [at_depth(s) for s in (1, 2, -1, -2)]
-    greeted += [at_plane(-(d // ny), -(d % ny)) for d in range(1, plane)]
+    greeted += [at_plane(0, -d) for d in range(1, ny)] + [at_plane(-d, 0) for d in range(1, nx)]
     for device in greeted:
         pl.semaphore_signal(barrier, inc=1, device_id=device, device_id_type=MESH)
 
@@ -219,27 +219,25 @@
     ]
     rounds = len(metas)
 
-    def to_plane(d):
+    def tiles_to(device, source, target, count, send_sem, recv_sem):
         return pltpu.make_async_remote_copy(
-            src_ref=right_panel.at[pl.ds(0, PAIRS)],
-            dst_ref=right_panel.at[pl.ds(d * PAIRS, PAIRS)],
-            send_sem=plane_send.at[d],
-            recv_sem=plane_recv.at[d],
-            device_id=at_plane(d // ny, lax.rem(d, ny)),
+            src_ref=right_panel.at[pl.ds(source * PAIRS, count * PAIRS)],
+            dst_ref=right_panel.at[pl.ds(target * PAIRS, count * PAIRS)],
+            send_sem=send_sem,
+            recv_sem=recv_sem,
+            device_id=device,
             device_id_type=MESH,
         )
 
-    def to_twin(d):
-        return pltpu.make_async_remote_copy(
-            src_ref=right_panel.at[pl.ds(d * PAIRS, PAIRS)],
-            dst_ref=right_panel.at[pl.ds((plane + d) * PAIRS, PAIRS)],
-            send_sem=twin_send.at[d],
-            recv_sem=twin_recv.at[d],
-            device_id=twin,
-            device_id_type=MESH,
-        )
-
-    group = -(-(plane - 1) // rounds)
+    along_y = [None] + [
+        tiles_to(at_plane(0, d), 0, d, 1, plane_send.at[d], plane_recv.at[d]) for d in range(1, ny)
+    ]
+    along_x = [None] + [
+        tiles_to(at_plane(d, 0), 0, d * ny, ny, plane_send.at[ny + d], plane_recv.at[ny + d]) for d in range(1, nx)
+    ]
+    to_twin = [
+        tiles_to(twin, d * ny, plane + d * ny, ny, twin_send.at[d], twin_recv.at[d]) for d in range(nx)
+    ]
 
     def beside(k):
         if 0 < k <= rounds:
@@ -247,17 +245,22 @@
         if k < rounds:
             metas[k].start()
         if k == 0:
-            to_twin(0).start()
-        for d in range(1 + (k - 1) * group, min(plane, 1 + k * group)):
-            if d > 0:
-                to_plane(d).wait_recv()
-                to_twin(d).start()
-        for d in range(1 + k * group, min(plane, 1 + (k + 1) * group)):
-            to_plane(d).start()
+            for copy in along_y[1:]:
+                copy.start()
+        if k == 1:
+            for copy in along_y[1:]:
+                copy.wait_recv()
+            for copy in along_x[1:]:
+                copy.start()
+            to_twin[0].start()
+        for d in range(1, nx):
+            if k == (5 if d == 2 else 4):
+                along_x[d].wait_recv()
+                to_twin[d].start()
 
     codes_copy = pltpu.make_async_copy(codes_vector, codes, codes_sem)
     first = (left_panel, left_meta, left_send, left_recv)
-    for k in range(max(stages, rounds + 1)):
+    for k in range(max(stages, rounds + 1, 6)):
         if k < stages:
             for p in (KEYS,) + pieces:
                 for way in range(2):
@@ -272,9 +275,8 @@
     codes_vector[16:32] = paired
     codes_copy.start()
 
-    @pl.loop(0, plane)
-    def _(d):
-        to_twin(d).wait_recv()
+    for copy in to_twin:
+        copy.wait_recv()
 
     codes_copy.wait()
 
@@ -310,7 +312,7 @@
             between_in(second, k - 1, pieces)
             sent(second, k - 1, pieces)
         sent(first, k, (KEYS,) + pieces)
-        for copy in (metas + [to_twin(d) for d in range(plane)] + [to_plane(d) for d in range(1, plane)])[k - 1 :: stages]:
+        for copy in (metas + to_twin + along_y[1:] + along_x[1:])[k - 1 :: stages]:
             copy.wait_send()
     last_in(second, pieces)
 

time: 120 us -> 116 us (0.967)
  the two profiles are of different devices: /device:TPU:32 before, /device:TPU:2 now
where the time goes in v5:
time: 116 us
  Pallas kernels  115 us (99%)
  local copies, waits for them, and re-layouts  1.72 us (1%)
    pallas_call x1, Pallas kernels, shards(): pl.pallas_call(functools.partial(kernel, nx, ny, nz), out_shape=jax.Shape...  115 us

profile of v5, /device:TPU:2, one launch (start us, length us, event | category | flops | bytes accessed | tf_op | source)
XLA Modules:
  0.0 116.3 jit_solution(6302214582257789648)
XLA Ops:
  0.0 114.6 %shard_map.37 = f32[10,64,64]{2,1,0:T(8,128)} custom-call(bf16[10,64,64]{2,1,0:T(8,128)(2,1)} %bitcast.5, s32[1,10]{1,0:T(1,128)} %bitcast.6, s32[1,10]{1,0:T(1,128)} %bitcast.7), custom_call_target="tpu_custom_call" | custom-call | tf_op jit(solution)/shard_map/pallas_call | solution.py:331
  114.6 1.7 %copy.5 = f32[1,1,10,64,64]{4,3,2,1,0:T(8,128)} copy(f32[1,1,10,64,64]{4,3,2,1,0:T(8,128)} %bitcast.4) | data formatting | bytes 327680
